TPU v7x, 32 devices: a whole 2x2x4 slice. The times are simulated.
32 devices in a mesh: groups: 2 (over y), head: 4 (over x, core), dp: 4 (over z).
Axes of the slice: x: 2, y: 2, z: 4, core: 2. Of those that a mesh axis runs over, the one named last changes fastest.
Arguments:
- queries: bfloat16 [8, 512, 12288], P(('groups', 'dp'), None, 'head'), parts along dimension 0, may hold values from -8 to 8
- out_grad: bfloat16 [8, 512, 8192], P(('groups', 'dp'), None, 'head'), parts along dimension 0, may hold values from -6 to 6
- latent: bfloat16 [8, 512, 576], P(('groups', 'dp'), 'head'), parts along dimension 0, may hold values from -8 to 8
- w_uk: bfloat16 [512, 8192], P(None, 'head'), may hold values from -0.25 to 0.25
- w_uv: bfloat16 [512, 8192], P(None, 'head'), may hold values from -0.25 to 0.25
- lengths: int32 [8], P(('groups', 'dp')), parts along dimension 0, may hold values from 128 to 512
- rewards: float32 [8], P('groups'), parts along dimension 0, may hold values from -6 to 6
- pairing: int32 [8], P('groups'), parts along dimension 0, may hold values from 0 to 3, each once
Outputs:
- q_grad: bfloat16 [8, 512, 12288], P(('groups', 'dp'), None, 'head'), parts along dimension 0
- latent_grad: bfloat16 [8, 512, 576], P(('groups', 'dp'), 'head'), parts along dimension 0
- uk_grad: float32 [1024, 8192], P(('groups', 'dp'), 'head'), parts along dimension 0
- uv_grad: float32 [1024, 8192], P(('groups', 'dp'), 'head'), parts along dimension 0
There are 2 independent parts, one for each index of `groups`. A program takes and returns all parts, laid end to end along the dimension named above; an argument that names none is the same for every part. Nothing has to cross between parts.
All inputs are finite; a program needn't handle non-finite values.
Results may differ from a plain program's by a relative error of at most 0.008.
Values may be sent and summed in bfloat16 or wider, within the bound.
A program may use at most 64 MiB of HBM per device.

v0:
```python
import jax
import jax.numpy as jnp
from jax import lax
from jax.sharding import PartitionSpec as P

L = 512
D_C = 512
D_R = 64
DN = 128
DV = 128


def pair_weights(rewards, pairing):
    count = pairing.shape[0]
    onehot = (pairing[:, None] == jnp.arange(count, dtype=jnp.int32)[None, :]).astype(jnp.float32)
    ordered = jnp.sum(onehot * rewards[None, :], axis=1)
    push = jax.nn.sigmoid(ordered[1::2] - ordered[0::2])
    in_order = jnp.stack([-push, push], axis=1).reshape(count)
    return jnp.sum(onehot * in_order[:, None], axis=0)


def head_backward(query_head, grad_head, key_head, value_head, rope_keys, valid):
    factor = (DN + D_R) ** (-0.5)
    scores = jnp.dot(query_head[:, :DN], key_head.T, preferred_element_type=jnp.float32)
    scores = scores + jnp.dot(query_head[:, DN:], rope_keys.T, preferred_element_type=jnp.float32)
    scores = jnp.where(valid, scores * factor, -1e30)
    top = jnp.max(scores, axis=1, keepdims=True)
    expo = jnp.exp(scores - top)
    prob = expo / jnp.sum(expo, axis=1, keepdims=True)
    prob_b = prob.astype(jnp.bfloat16)
    dprob = jnp.dot(grad_head, value_head.T, preferred_element_type=jnp.float32)
    delta = jnp.sum(prob * dprob, axis=1, keepdims=True)
    dscore = (prob * (dprob - delta)).astype(jnp.bfloat16)
    dq_nope = jnp.dot(dscore, key_head, preferred_element_type=jnp.float32)
    dq_rope = jnp.dot(dscore, rope_keys, preferred_element_type=jnp.float32)
    dquery = (jnp.concatenate([dq_nope, dq_rope], axis=1) * factor).astype(jnp.bfloat16)
    dkey = (
        jnp.dot(dscore.T, query_head[:, :DN], preferred_element_type=jnp.float32) * factor
    ).astype(jnp.bfloat16)
    drope = jnp.dot(dscore.T, query_head[:, DN:], preferred_element_type=jnp.float32) * factor
    dvalue = jnp.dot(prob_b.T, grad_head, preferred_element_type=jnp.float32).astype(jnp.bfloat16)
    return (dquery, dkey, dvalue, drope)


def sequence_attention(query_rows, grad_rows, keys, values, rope_keys, length, weight, heads):
    where = jnp.arange(L, dtype=jnp.int32)
    valid = (where[None, :] <= where[:, None]) & (where[None, :] < length)
    rowmask = (where < length).astype(jnp.float32)
    scaled = (grad_rows.astype(jnp.float32) * weight * rowmask[:, None]).astype(jnp.bfloat16)
    query_heads = query_rows.reshape(L, heads, DN + D_R).transpose(1, 0, 2)
    grad_heads = scaled.reshape(L, heads, DV).transpose(1, 0, 2)
    key_heads = keys.reshape(L, heads, DN).transpose(1, 0, 2)
    value_heads = values.reshape(L, heads, DV).transpose(1, 0, 2)

    def one_head(items):
        return head_backward(items[0], items[1], items[2], items[3], rope_keys, valid)

    dquery, dkey, dvalue, drope = lax.map(
        one_head, (query_heads, grad_heads, key_heads, value_heads)
    )
    dquery = dquery.transpose(1, 0, 2).reshape(L, heads * (DN + D_R))
    dkey = dkey.transpose(1, 0, 2).reshape(L, heads * DN)
    dvalue = dvalue.transpose(1, 0, 2).reshape(L, heads * DV)
    return (dquery, dkey, dvalue, jnp.sum(drope, axis=0))


def on_device(queries, out_grad, latent, w_uk, w_uv, lengths, rewards, pairing):
    seq_dev = queries.shape[0]
    heads_dev = w_uk.shape[1] // DN
    key_width = heads_dev * DN
    lat_width = D_C + D_R
    weights_all = pair_weights(rewards, pairing)
    own_weights = lax.dynamic_slice_in_dim(weights_all, lax.axis_index("dp") * seq_dev, seq_dev)
    piece = lax.all_gather(latent, "head", axis=1, tiled=True)
    content = piece[:, :, :D_C]
    keys = jnp.einsum("srk,kn->srn", content, w_uk, preferred_element_type=jnp.float32).astype(
        jnp.bfloat16
    )
    values = jnp.einsum("srk,kn->srn", content, w_uv, preferred_element_type=jnp.float32).astype(
        jnp.bfloat16
    )
    full = jnp.concatenate([piece, keys, values], axis=2)
    index = 0
    content = full[index, :, :D_C]
    rope_keys = full[index, :, D_C:lat_width]
    keys = full[index, :, lat_width : lat_width + key_width]
    values = full[index, :, lat_width + key_width :]
    dquery, dkey, dvalue, drope = sequence_attention(
        queries[index],
        out_grad[index],
        keys,
        values,
        rope_keys,
        lengths[index],
        own_weights[index],
        heads_dev,
    )
    query_grads = [dquery]
    key_grads = [dkey]
    value_grads = [dvalue]
    rope_grads = [drope]
    q_grad = jnp.stack(query_grads, axis=0)
    stacked_keys = key_grads[0]
    stacked_values = value_grads[0]
    index = 0
    dcontent = lax.dot_general(
        key_grads[index], w_uk, (((1,), (1,)), ((), ())), preferred_element_type=jnp.float32
    )
    dcontent = dcontent + lax.dot_general(
        value_grads[index], w_uv, (((1,), (1,)), ((), ())), preferred_element_type=jnp.float32
    )
    terms = [jnp.concatenate([dcontent, rope_grads[index]], axis=1)]
    partial_sums = jnp.stack(terms, axis=0)
    latent_grad = lax.psum_scatter(partial_sums, "head", scatter_dimension=1, tiled=True).astype(
        jnp.bfloat16
    )
    both = jnp.concatenate([stacked_keys, stacked_values], axis=1)
    owned = lax.psum_scatter(
        lax.dot_general(
            content, both, (((0,), (0,)), ((), ())), preferred_element_type=jnp.float32
        ),
        "dp",
        scatter_dimension=0,
        tiled=True,
    )
    uk_grad = owned[:, :key_width]
    uv_grad = owned[:, key_width:]
    return (q_grad, latent_grad, uk_grad, uv_grad)


def solution(mesh):
    in_specs = (
        P(("groups", "dp"), None, "head"),
        P(("groups", "dp"), None, "head"),
        P(("groups", "dp"), "head", None),
        P(None, "head"),
        P(None, "head"),
        P(("groups", "dp")),
        P("groups"),
        P("groups"),
    )
    out_specs = (
        P(("groups", "dp"), None, "head"),
        P(("groups", "dp"), "head", None),
        P(("groups", "dp"), "head"),
        P(("groups", "dp"), "head"),
    )
    return jax.shard_map(
        on_device, mesh=mesh, in_specs=in_specs, out_specs=out_specs, check_vma=False
    )
```

profile of v0, /device:TPU:6, one launch (start us, length us, event | category | flops | bytes accessed | tf_op | source)
XLA Modules:
  0.0 458.4 jit_solution(5672848975666087731)
XLA Ops:
  11.1 7.5 %all_gather.3 = bf16[1,512,576]{2,1,0:T(8,128)(2,1)S(1)} all-gather(bf16[1,128,576]{2,1,0:T(8,128)(2,1)S(1)} %copy.33), channel_id=1, replica_groups=mesh['groups'=2,'head'=4,'dp'=4] {'head'}, dimensions={1}, use_global_device_ids=true | all-gather | bytes 737280 | tf_op jit(solution)/shard_map/all_gather | solution.py:74
  18.6 4.5 fusion.41
  23.1 2.6 fusion.40
  25.7 3.9 copy.35
  29.6 4.6 %copy.32 = bf16[1,512,3072]{1,2,0:T(8,128)(2,1)} copy(bf16[1,512,3072]{2,1,0:T(8,128)(2,1)} %param.10) | data formatting | bytes 6291456 | tf_op args[0]
  34.8 5.4 %bitcast_bitcast_fusion = (bf16[16,512,128]{2,1,0:T(8,128)(2,1)}, bf16[16,512,128]{2,1,0:T(8,128)(2,1)}) fusion(bf16[64,16,8,128]{3,2,1,0:T(8,128)(2,1)} %fusion.41, bf16[64,16,8,128]{3,2,1,0:T(8,128)(2,1)} %fusion.40), kind=kLoop, calls=%fused_computation.57 | loop fusion | bytes 8388608 | tf_op jit(solution)/shard_map/transpose | solution.py:53
  41.5 1.9 fusion.39
  43.4 217.2 %while.17 = (s32[]{:T(128)}, bf16[16,512,192]{1,2,0:T(8,128)(2,1)}, bf16[16,512,128]{1,2,0:T(8,128)(2,1)}, bf16[16,512,128]{1,2,0:T(8,128)(2,1)}, f32[16,512,64]...) while((s32[]{:T(128)}, bf16[16,512,192]{1,2,0:T(8,128)(2,1)}, ...), condition=%wide.region_6.7_spmd.clone, body=%wide.region_2.6_spmd.clone.sunk | while | flops 441973248 | bytes 21389008 | solution.py:58
  46.3 2.0 fusion.96
  48.3 1.7 copy.59
  51.3 1.5 multiply_convert_fusion.3
  59.8 2.0 fusion.96
  61.9 1.7 copy.59
  64.8 1.5 multiply_convert_fusion.3
  73.4 2.0 fusion.96
  75.5 1.7 copy.59
  78.4 1.5 multiply_convert_fusion.3
  87.0 2.0 fusion.96
  89.0 1.7 copy.59
  92.0 1.5 multiply_convert_fusion.3
  100.6 2.0 fusion.96
  102.6 1.7 copy.59
  105.5 1.5 multiply_convert_fusion.3
  114.1 2.0 fusion.96
  116.2 1.7 copy.59
  119.1 1.5 multiply_convert_fusion.3
  127.7 2.0 fusion.96
  129.8 1.7 copy.59
  132.7 1.5 multiply_convert_fusion.3
  141.3 2.0 fusion.96
  143.3 1.7 copy.59
  146.2 1.5 multiply_convert_fusion.3
  154.9 2.0 fusion.96
  156.9 1.7 copy.59
  159.8 1.5 multiply_convert_fusion.3
  168.4 2.0 fusion.96
  170.5 1.7 copy.59
  173.4 1.5 multiply_convert_fusion.3
  182.0 2.0 fusion.96
  184.0 1.7 copy.59
  187.0 1.5 multiply_convert_fusion.3
  195.6 2.0 fusion.96
  197.6 1.7 copy.59
  200.6 1.5 multiply_convert_fusion.3
  209.2 2.0 fusion.96
  211.2 1.7 copy.59
  214.1 1.5 multiply_convert_fusion.3
  222.7 2.0 fusion.96
  224.8 1.7 copy.59
  227.7 1.5 multiply_convert_fusion.3
  236.3 2.0 fusion.96
  238.4 1.7 copy.59
  249.9 2.0 fusion.96
  251.9 1.7 copy.59
  260.6 3.8 fusion.46
  264.4 1.8 reduce_sum.47
  266.2 3.7 convolution_add_fusion.1
  271.3 7.8 %convolution_bitcast_fusion.2 = f32[512,4096]{0,1:T(8,128)} fusion(bf16[512,2048]{0,1:T(8,128)(2,1)} %bitcast.131, bf16[512,2048]{0,1:T(8,128)(2,1)} %bitcast.133, bf16[1,512,576]{2,1,0:T(8,128)(2,1)S(1)} %copy-done.5), kind=kOutput, calls=%fused_computation.48 | convolution fusion | flops 2155872256 | bytes 13107200 | tf_op jit(solution)/shard_map/dot_general | solution.py:119
  279.1 4.7 %copy.42 = bf16[1,512,3072]{2,1,0:T(8,128)(2,1)} copy(bf16[1,512,3072]{1,2,0:T(8,128)(2,1)} %bitcast.128) | data formatting | bytes 6291456
  283.8 13.4 %reduce-scatter.3.cloned.1.call-done = f32[1,128,576]{1,2,0:T(8,128)} async-done(((f32[1,512,576]{1,2,0:T(8,128)}), f32[1,128,576]{1,2,0:T(8,128)}) %reduce-scatter.3.cloned.1.call-update) | async-done | bytes 294928 | tf_op jit(solution)/shard_map/reduce_scatter | solution.py:114
  297.2 1.6 convert_element_type.55
  298.9 146.3 %reduce-scatter.5.cloned.1.call-done = f32[128,4096]{0,1:T(8,128)} async-done(((f32[512,4096]{0,1:T(8,128)}), f32[128,4096]{0,1:T(8,128)}) %reduce-scatter.5.cloned.1.call-update) | async-done | bytes 2097168 | tf_op jit(solution)/shard_map/reduce_scatter | solution.py:118
  445.1 2.6 fusion.45
  447.8 2.5 copy.44
  (305 shorter events, 143.6 us)
Async XLA Ops:
  7.2 15.9 %copy-start = (bf16[512,2048]{1,0:T(8,128)(2,1)S(1)}, bf16[512,2048]{1,0:T(8,128)(2,1)}, u32[]{:S(2)}) copy-start(bf16[512,2048]{1,0:T(8,128)(2,1)} %param.13) | copy-start | bytes 6291460
  7.2 290.0 %reduce-scatter.3.cloned.1.call-start = ((), (), s32[]{:S(2)}) async-start(), calls=%async_computation.2 | async-start | bytes 1474560 | tf_op jit(solution)/shard_map/reduce_scatter | solution.py:114
  18.6 4.5 copy-start.4
  34.8 5.4 %copy-start.3 = (bf16[1,512,2048]{1,2,0:T(8,128)(2,1)S(1)}, bf16[1,512,2048]{1,2,0:T(8,128)(2,1)}, u32[]{:S(2)}) copy-start(bf16[1,512,2048]{1,2,0:T(8,128)(2,1)} %copy.35) | copy-start | bytes 6291460
  46.1 3.9 copy-start.1
  52.8 3.5 copy-start.2
  59.6 3.9 copy-start.1
  66.3 3.5 copy-start.2
  73.2 3.9 copy-start.1
  79.9 3.5 copy-start.2
  86.8 3.9 copy-start.1
  93.5 3.5 copy-start.2
  100.4 3.9 copy-start.1
  107.1 3.5 copy-start.2
  113.9 3.9 copy-start.1
  120.6 3.5 copy-start.2
  127.5 3.9 copy-start.1
  134.2 3.5 copy-start.2
  141.0 3.9 copy-start.1
  147.7 3.5 copy-start.2
  154.6 3.9 copy-start.1
  161.3 3.5 copy-start.2
  168.2 3.9 copy-start.1
  174.9 3.5 copy-start.2
  181.8 3.9 copy-start.1
  188.5 3.5 copy-start.2
  195.4 3.9 copy-start.1
  202.1 3.5 copy-start.2
  209.0 3.9 copy-start.1
  215.6 3.5 copy-start.2
  222.5 3.9 copy-start.1
  229.2 3.5 copy-start.2
  236.1 3.9 copy-start.1
  242.8 3.5 copy-start.2
  249.7 3.9 copy-start.1
  256.4 3.5 copy-start.2
  269.9 1.4 copy-start.5
  271.1 174.0 %reduce-scatter.5.cloned.1.call-start = ((), (), s32[]{:S(2)}) async-start(), calls=%async_computation.3 | async-start | bytes 10485760 | tf_op jit(solution)/shard_map/reduce_scatter | solution.py:118
Sparse Core Ops, SparseCore 0:
  271.2 25.9 reduce-scatter.2
  299.7 145.3 reduce-scatter.4
where the time goes:
time: 463 us; the launch traced here: 458 us
  waiting for transfers between devices  160 us (35%)
  matrix products  143 us (31%)
  local copies, waits for them, and re-layouts  84.4 us (18%)
  other arithmetic  48 us (10%)
  between operations  14.8 us (3%)
  blocking collectives  7.49 us (2%)
    reduce_scatter x1, waiting for transfers between devices, on_device(): lax.psum_scatter(lax.dot_general(content, both, (((0,), (0,)), ((), ())),...  146 us
    dynamic_update_slice x48, local copies, waits for them, and re-layouts, sequence_attention(): lax.map(one_head, (query_heads, grad_heads, key_heads, value_heads))  39.8 us
    dot_general x16, matrix products, head_backward(): jnp.dot(prob_b.T, grad_head, preferred_element_type=jnp.float32)  32.7 us
    convert_element_type x16, other arithmetic, head_backward(): dscore = (prob * (dprob - delta)).astype(jnp.bfloat16)  24.1 us
    dot_general x16, matrix products, head_backward(): dprob = jnp.dot(grad_head, value_head.T, preferred_element_type=jnp.float32)  20.4 us
    dot_general x16, matrix products, head_backward(): jnp.dot(query_head[:, :DN], key_head.T, preferred_element_type=jnp.float32)  19.2 us
    dot_general x16, matrix products, head_backward(): dq_nope = jnp.dot(dscore, key_head, preferred_element_type=jnp.float32)  18.8 us
    unnamed x14, local copies, waits for them, and re-layouts  18.2 us
  transfers between devices with their start and end apart: 2, of which 2 were waited for; matrix products, arithmetic and copies ran while one was open for 3% of the time, Pallas kernels for 0%

commit v1 on v0

v1 whole, which is shorter than its diff:
```python
import functools

import jax
import jax.numpy as jnp
from jax import lax
from jax.experimental import pallas as pl
from jax.experimental.pallas import tpu as pltpu
from jax.sharding import PartitionSpec as P

D_C = 512
D_R = 64
DN = 128
DV = 128
BLK = 256
MESH = pl.DeviceIdType.MESH
F32 = jnp.float32
BF16 = jnp.bfloat16


def dot_nn(a, b):
    return lax.dot_general(a, b, (((1,), (0,)), ((), ())), preferred_element_type=F32)


def dot_nt(a, b):
    return lax.dot_general(a, b, (((1,), (1,)), ((), ())), preferred_element_type=F32)


def dot_tn(a, b):
    return lax.dot_general(a, b, (((0,), (0,)), ((), ())), preferred_element_type=F32)


def own_weight(rewards, pairing, own):
    count = rewards.shape[0]
    diff = jnp.float32(0.0)
    sign = jnp.float32(0.0)
    for k in range(count // 2):
        chosen, rejected = pairing[2 * k], pairing[2 * k + 1]
        gap = jnp.float32(0.0)
        for j in range(count):
            gap = gap + jnp.where(rejected == j, rewards[j], 0.0)
            gap = gap - jnp.where(chosen == j, rewards[j], 0.0)
        diff = jnp.where((chosen == own) | (rejected == own), gap, diff)
        sign = jnp.where(chosen == own, -1.0, jnp.where(rejected == own, 1.0, sign))
    return sign * jax.nn.sigmoid(jnp.full((1, DV), diff, F32))


def kernel(
    n_head, n_dp, pairs,
    lengths, rewards, pairing, latent, q, og, wk, wv,
    qg, lg, uk, uv,
    full, cont_t, send, recv, dkv, rope_acc, lacc, lrecv,
    g_send, g_recv, p_send, p_recv, l_send, l_recv,
):
    factor = (DN + D_R) ** (-0.5)
    me_h = lax.axis_index("head")
    me_d = lax.axis_index("dp")
    tokens = latent.shape[0]
    length_all = full.shape[0]
    blocks = length_all // BLK

    barrier = pltpu.get_barrier_semaphore()
    for o in range(1, n_head):
        pl.semaphore_signal(
            barrier, inc=1, device_id={"head": lax.rem(me_h + o, n_head)}, device_id_type=MESH
        )
    for o in range(1, n_dp):
        pl.semaphore_signal(
            barrier, inc=1, device_id={"dp": lax.rem(me_d + o, n_dp)}, device_id_type=MESH
        )
    pl.semaphore_wait(barrier, n_head + n_dp - 2)

    own_rows = pl.ds(pl.multiple_of(me_h * tokens, tokens), tokens)

    def gather(o):
        return pltpu.make_async_remote_copy(
            src_ref=latent,
            dst_ref=full.at[own_rows],
            send_sem=g_send.at[o - 1],
            recv_sem=g_recv.at[o - 1],
            device_id={"head": lax.rem(me_h + o, n_head)},
            device_id_type=MESH,
        )

    def partial(p, o):
        peer = lax.rem(me_d + o, n_dp)
        return pltpu.make_async_remote_copy(
            src_ref=send.at[p, peer],
            dst_ref=recv.at[p, o - 1],
            send_sem=p_send.at[p, o - 1],
            recv_sem=p_recv.at[p, o - 1],
            device_id={"dp": peer},
            device_id_type=MESH,
        )

    def latent_part(o):
        peer = lax.rem(me_h + o, n_head)
        return pltpu.make_async_remote_copy(
            src_ref=lacc.at[peer],
            dst_ref=lrecv.at[o - 1],
            send_sem=l_send.at[o - 1],
            recv_sem=l_recv.at[o - 1],
            device_id={"head": peer},
            device_id_type=MESH,
        )

    for o in range(1, n_head):
        gather(o).start()
    full[own_rows, :] = latent[...]
    length = lengths[0]
    weight = own_weight(rewards, pairing, me_d)
    rope_acc[...] = jnp.zeros_like(rope_acc)
    for o in range(1, n_head):
        gather(o).wait()
    cont_t[...] = full[:, :D_C].T

    def body(p, carry):
        cols = pl.ds(pl.multiple_of(p * 2 * DN, 2 * DN), 2 * DN)
        qcols = pl.ds(pl.multiple_of(p * 2 * (DN + D_R), 2 * (DN + D_R)), 2 * (DN + D_R))
        content = full[:, :D_C]
        rope = full[:, D_C:]
        k2 = dot_nn(content, wk[:, cols]).astype(BF16)
        v2 = dot_nn(content, wv[:, cols]).astype(BF16)
        empty = jnp.zeros((length_all, D_R), BF16)
        keys = (
            jnp.concatenate([k2[:, :DN], rope, empty], axis=1),
            jnp.concatenate([empty, k2[:, DN:], rope], axis=1),
        )
        row = lax.broadcasted_iota(jnp.int32, (length_all, 2 * DV), 0)
        w2 = jnp.concatenate([weight, weight], axis=1)
        g2 = og[:, cols].astype(F32) * w2
        g2 = jnp.where(row < length, g2, 0.0).astype(BF16)
        dks, dvs = [], []
        dqs = [[], []]
        for side in range(2):
            kx = keys[side]
            vx = v2[:, side * DV : (side + 1) * DV]
            dk = [None] * blocks
            dv = [None] * blocks
            for b in range(blocks):
                reach = (b + 1) * BLK
                rows = slice(b * BLK, reach)
                qx = q[rows, qcols][:, side * DN : side * DN + 2 * DN]
                gx = g2[rows, side * DV : (side + 1) * DV]
                at_j = lax.broadcasted_iota(jnp.int32, (reach, BLK), 0)
                at_i = lax.broadcasted_iota(jnp.int32, (reach, BLK), 1) + b * BLK
                valid = (at_j <= at_i) & (at_j < length)
                score = jnp.where(valid, dot_nt(kx[:reach], qx) * factor, -1e30)
                top = jnp.max(score, axis=0, keepdims=True)
                expo = jnp.exp(score - top)
                prob = expo * (1.0 / jnp.sum(expo, axis=0, keepdims=True))
                dprob = dot_nt(vx[:reach], gx)
                delta = jnp.sum(prob * dprob, axis=0, keepdims=True)
                dscore = (prob * (dprob - delta)).astype(BF16)
                dqs[side].append(dot_tn(dscore, kx[:reach]))
                dk_b = dot_nn(dscore, qx)
                dv_b = dot_nn(prob.astype(BF16), gx)
                for j in range(b + 1):
                    part = slice(j * BLK, (j + 1) * BLK)
                    dk[j] = dk_b[part] if dk[j] is None else dk[j] + dk_b[part]
                    dv[j] = dv_b[part] if dv[j] is None else dv[j] + dv_b[part]
            dks.append(jnp.concatenate(dk, axis=0) * factor)
            dvs.append(jnp.concatenate(dv, axis=0))
        for b in range(blocks):
            left, right = dqs[0][b], dqs[1][b]
            dq = jnp.concatenate(
                [left[:, :DN], left[:, DN:] + right[:, :DN], right[:, DN:]], axis=1
            )
            qg[b * BLK : (b + 1) * BLK, qcols] = (dq * factor).astype(BF16)
        rope_acc[:, :DN] += dks[0][:, DN:]
        rope_acc[:, DN:] += dks[1][:, DN:]
        both = jnp.concatenate(
            [
                dks[0][:, :DN].astype(BF16),
                dks[1].astype(BF16)[:, D_R : D_R + DN],
                dvs[0].astype(BF16),
                dvs[1].astype(BF16),
            ],
            axis=1,
        )
        dkv[p] = both
        sums = dot_nn(cont_t[...], both).astype(BF16)
        send[p] = sums.reshape(n_dp, D_C // n_dp, 2 * DN + 2 * DV)
        for o in range(1, n_dp):
            partial(p, o).start()
        return carry

    lax.fori_loop(0, pairs, body, 0)

    lacc[:, :, D_C:] = (
        (rope_acc[:, :D_R] + rope_acc[:, DN + D_R :])
    ).reshape(n_head, tokens, D_R)
    lacc[:, :, :D_C] = jnp.zeros((n_head, tokens, D_C), F32)

    def back(p, carry):
        cols = pl.ds(pl.multiple_of(p * 2 * DN, 2 * DN), 2 * DN)
        term = dot_nt(dkv[p, :, : 2 * DN], wk[:, cols]) + dot_nt(dkv[p, :, 2 * DN :], wv[:, cols])
        lacc[:, :, :D_C] += term.reshape(n_head, tokens, D_C)
        return carry

    lax.fori_loop(0, pairs, back, 0)
    for o in range(1, n_head):
        latent_part(o).start()
    total = lacc[me_h]
    for o in range(1, n_head):
        latent_part(o).wait()
        total = total + lrecv[o - 1]
    lg[...] = total.astype(BF16)

    def finish(p, carry):
        cols = pl.ds(pl.multiple_of(p * 2 * DN, 2 * DN), 2 * DN)
        total = send[p, me_d].astype(F32)
        for o in range(1, n_dp):
            partial(p, o).wait()
            total = total + recv[p, o - 1].astype(F32)
        uk[:, cols] = total[:, : 2 * DN]
        uv[:, cols] = total[:, 2 * DN :]
        return carry

    lax.fori_loop(0, pairs, finish, 0)


def on_device(n_head, n_dp, queries, out_grad, latent, w_uk, w_uv, lengths, rewards, pairing):
    _, length_all, q_width = queries.shape
    tokens = latent.shape[1]
    key_width = w_uk.shape[1]
    pairs = key_width // (2 * DN)
    rows = D_C // n_dp
    vmem = pl.BlockSpec(memory_space=pltpu.VMEM)
    smem = pl.BlockSpec(memory_space=pltpu.SMEM)
    q_grad, latent_grad, uk_grad, uv_grad = pl.pallas_call(
        functools.partial(kernel, n_head, n_dp, pairs),
        out_shape=(
            jax.ShapeDtypeStruct((length_all, q_width), BF16),
            jax.ShapeDtypeStruct((tokens, D_C + D_R), BF16),
            jax.ShapeDtypeStruct((rows, key_width), F32),
            jax.ShapeDtypeStruct((rows, key_width), F32),
        ),
        in_specs=[smem] * 3 + [vmem] * 5,
        out_specs=(vmem,) * 4,
        scratch_shapes=[
            pltpu.VMEM((length_all, D_C + D_R), BF16),
            pltpu.VMEM((D_C, length_all), BF16),
            pltpu.VMEM((pairs, n_dp, rows, 2 * DN + 2 * DV), BF16),
            pltpu.VMEM((pairs, n_dp - 1, rows, 2 * DN + 2 * DV), BF16),
            pltpu.VMEM((pairs, length_all, 2 * DN + 2 * DV), BF16),
            pltpu.VMEM((length_all, 2 * DN), F32),
            pltpu.VMEM((n_head, tokens, D_C + D_R), F32),
            pltpu.VMEM((n_head - 1, tokens, D_C + D_R), F32),
            pltpu.SemaphoreType.DMA((n_head - 1,)),
            pltpu.SemaphoreType.DMA((n_head - 1,)),
            pltpu.SemaphoreType.DMA((pairs, n_dp - 1)),
            pltpu.SemaphoreType.DMA((pairs, n_dp - 1)),
            pltpu.SemaphoreType.DMA((n_head - 1,)),
            pltpu.SemaphoreType.DMA((n_head - 1,)),
        ],
        compiler_params=pltpu.CompilerParams(
            collective_id=0, has_side_effects=True, vmem_limit_bytes=52 * 1024 * 1024
        ),
    )(lengths, rewards, pairing, latent[0], queries[0], out_grad[0], w_uk, w_uv)
    return q_grad[None], latent_grad[None], uk_grad, uv_grad


def solution(mesh):
    in_specs = (
        P(("groups", "dp"), None, "head"),
        P(("groups", "dp"), None, "head"),
        P(("groups", "dp"), "head", None),
        P(None, "head"),
        P(None, "head"),
        P(("groups", "dp")),
        P("groups"),
        P("groups"),
    )
    out_specs = (
        P(("groups", "dp"), None, "head"),
        P(("groups", "dp"), "head", None),
        P(("groups", "dp"), "head"),
        P(("groups", "dp"), "head"),
    )
    return jax.shard_map(
        functools.partial(on_device, mesh.shape["head"], mesh.shape["dp"]),
        mesh=mesh,
        in_specs=in_specs,
        out_specs=out_specs,
        check_vma=False,
    )
```

time: 463 us -> 122 us (0.26)
  the two profiles are of different devices: /device:TPU:6 before, /device:TPU:9 now
where the time goes in v1:
time: 122 us
  Pallas kernels  112 us (92%)
  local copies, waits for them, and re-layouts  8.95 us (7%)
  between operations  1.3 us (1%)
    pallas_call x1, Pallas kernels, on_device(): pl.pallas_call(functools.partial(kernel, n_head, n_dp, pairs), out_shape=...  112 us
    unnamed x11, local copies, waits for them, and re-layouts  8.95 us

profile of v1, /device:TPU:9, one launch (start us, length us, event | category | flops | bytes accessed | tf_op | source)
XLA Modules:
  0.0 121.9 jit_solution(15830695286706734578)
XLA Ops:
  1.3 1.1 copy.12
  2.3 0.0 copy-start
  2.4 0.6 copy-done
  3.0 0.0 copy-start.1
  3.0 0.7 copy-done.1
  3.7 111.7 %shard_map.111 = (bf16[512,3072]{1,0:T(8,128)(2,1)}, bf16[128,576]{1,0:T(8,128)(2,1)S(1)}, f32[128,2048]{1,0:T(8,128)S(1)}, f32[128,2048]{1,0:T(8,128)}) custom-call(s32[1]{0:T(128)S(6)} %copy.17.lengths, f32[4]{0:T(128)S(1)} %copy-done, s32[4]{0:T(128)S(1)} %copy-done.1, bf16[128,576]{1,0:T(8,128)(2,1)S(1)} %bitcast.5, bf16[512,3072]{1,0:T(8,128)(2,1)} %bitcast.7, ...), custom_call_target="tpu_custom_call" | custom-call | tf_op jit(solution)/shard_map/pallas_call | solution.py:230
  115.3 0.8 copy.13
  116.1 0.0 copy-start.2
  116.1 3.8 %copy.18 = bf16[1,512,3072]{2,1,0:T(8,128)(2,1)} copy(bf16[1,512,3072]{2,1,0:T(8,128)(2,1)} %bitcast.8) | data formatting | bytes 6291456
  120.0 1.0 copy.19
  120.9 0.0 copy-done.2
  120.9 1.0 copy.20
Async XLA Ops:
  2.3 0.7 copy-start
  3.0 0.7 copy-start.1
  116.1 4.8 %copy-start.2 = (f32[128,2048]{1,0:T(8,128)S(1)}, f32[128,2048]{1,0:T(8,128)}, u32[]{:S(2)}) copy-start(f32[128,2048]{1,0:T(8,128)} %get-tuple-element.23) | copy-start | bytes 3145732

commit v2 on v1

--- a/solution.py
+++ b/solution.py
@@ -46,10 +46,10 @@
 
 def kernel(
     n_head, n_dp, pairs,
-    lengths, rewards, pairing, latent, q, og, wk, wv,
-    qg, lg, uk, uv,
-    full, cont_t, send, recv, dkv, rope_acc, lacc, lrecv,
-    g_send, g_recv, p_send, p_recv, l_send, l_recv,
+    lengths, rewards, pairing, latent, q_in, og_in, wk_in, wv_in,
+    qg_out, lg, uk, uv,
+    q, og, wk, wv, qg, full, cont_t, send, recv, dkv, rope_acc, lacc, lrecv,
+    g_send, g_recv, p_send, p_recv, l_send, l_recv, load_sem,
 ):
     factor = (DN + D_R) ** (-0.5)
     me_h = lax.axis_index("head")
@@ -57,17 +57,24 @@
     tokens = latent.shape[0]
     length_all = full.shape[0]
     blocks = length_all // BLK
+    last = 2
+    loads = [
+        pltpu.make_async_copy(src, dst, load_sem.at[n])
+        for n, (src, dst) in enumerate(((wk_in, wk), (wv_in, wv), (og_in, og), (q_in, q)))
+    ]
+    for load in loads:
+        load.start()
 
     barrier = pltpu.get_barrier_semaphore()
     for o in range(1, n_head):
         pl.semaphore_signal(
             barrier, inc=1, device_id={"head": lax.rem(me_h + o, n_head)}, device_id_type=MESH
         )
-    for o in range(1, n_dp):
+    for o in (1, n_dp - 1):
         pl.semaphore_signal(
             barrier, inc=1, device_id={"dp": lax.rem(me_d + o, n_dp)}, device_id_type=MESH
         )
-    pl.semaphore_wait(barrier, n_head + n_dp - 2)
+    pl.semaphore_wait(barrier, n_head + 1)
 
     own_rows = pl.ds(pl.multiple_of(me_h * tokens, tokens), tokens)
 
@@ -81,16 +88,34 @@
             device_id_type=MESH,
         )
 
-    def partial(p, o):
-        peer = lax.rem(me_d + o, n_dp)
+    steps = (lax.rem(me_d + 1, n_dp), lax.rem(me_d + n_dp - 1, n_dp))
+
+    def hop(p, d, way):
         return pltpu.make_async_remote_copy(
-            src_ref=send.at[p, peer],
-            dst_ref=recv.at[p, o - 1],
-            send_sem=p_send.at[p, o - 1],
-            recv_sem=p_recv.at[p, o - 1],
-            device_id={"dp": peer},
+            src_ref=send.at[p, d],
+            dst_ref=recv.at[p, way, d],
+            send_sem=p_send.at[p, d],
+            recv_sem=p_recv.at[p, way, d],
+            device_id={"dp": steps[way]},
             device_id_type=MESH,
         )
+
+    def forward(p, way):
+        order = range(n_dp - 1, 0, -1) if way == 0 else range(n_dp - 1)
+        for d in order:
+
+            @pl.when((me_d < d) if way == 0 else (me_d > d))
+            def _():
+                @pl.when((me_d > 0) if way == 0 else (me_d < n_dp - 1))
+                def _():
+                    hop(p, d, way).wait_recv()
+                    total = send[p, d].astype(F32) + recv[p, way, d].astype(F32)
+                    send[p, d] = total.astype(BF16)
+
+                hop(p, d, way).start()
+
+    place = (me_d, n_dp - 1 - me_d)
+    lags = tuple(at + (at + n_dp - 1) // n_dp for at in place)
 
     def latent_part(o):
         peer = lax.rem(me_h + o, n_head)
@@ -112,6 +137,8 @@
     for o in range(1, n_head):
         gather(o).wait()
     cont_t[...] = full[:, :D_C].T
+    for load in loads:
+        load.wait()
 
     def body(p, carry):
         cols = pl.ds(pl.multiple_of(p * 2 * DN, 2 * DN), 2 * DN)
@@ -180,11 +207,17 @@
         dkv[p] = both
         sums = dot_nn(cont_t[...], both).astype(BF16)
         send[p] = sums.reshape(n_dp, D_C // n_dp, 2 * DN + 2 * DV)
-        for o in range(1, n_dp):
-            partial(p, o).start()
+        for way in range(2):
+
+            @pl.when(p >= lags[way])
+            def _():
+                forward(p - lags[way], way)
+
         return carry
 
     lax.fori_loop(0, pairs, body, 0)
+    store = pltpu.make_async_copy(qg, qg_out, load_sem.at[0])
+    store.start()
 
     lacc[:, :, D_C:] = (
         (rope_acc[:, :D_R] + rope_acc[:, DN + D_R :])
@@ -195,11 +228,24 @@
         cols = pl.ds(pl.multiple_of(p * 2 * DN, 2 * DN), 2 * DN)
         term = dot_nt(dkv[p, :, : 2 * DN], wk[:, cols]) + dot_nt(dkv[p, :, 2 * DN :], wv[:, cols])
         lacc[:, :, :D_C] += term.reshape(n_head, tokens, D_C)
+        for way in range(2):
+
+            @pl.when((p + lags[way] >= pairs) & (p < pairs - last))
+            def _():
+                forward(p, way)
+
         return carry
 
     lax.fori_loop(0, pairs, back, 0)
     for o in range(1, n_head):
         latent_part(o).start()
+    for p in range(pairs - last, pairs):
+        for way in range(2):
+
+            @pl.when(p + lags[way] >= pairs)
+            def _():
+                forward(p, way)
+
     total = lacc[me_h]
     for o in range(1, n_head):
         latent_part(o).wait()
@@ -209,14 +255,27 @@
     def finish(p, carry):
         cols = pl.ds(pl.multiple_of(p * 2 * DN, 2 * DN), 2 * DN)
         total = send[p, me_d].astype(F32)
-        for o in range(1, n_dp):
-            partial(p, o).wait()
-            total = total + recv[p, o - 1].astype(F32)
         uk[:, cols] = total[:, : 2 * DN]
         uv[:, cols] = total[:, 2 * DN :]
+        for way in range(2):
+
+            @pl.when(place[way] > 0)
+            def _():
+                hop(p, me_d, way).wait_recv()
+                more = recv[p, way, me_d].astype(F32)
+                uk[:, cols] += more[:, : 2 * DN]
+                uv[:, cols] += more[:, 2 * DN :]
+
+            for d in range(n_dp):
+
+                @pl.when((me_d < d) if way == 0 else (me_d > d))
+                def _():
+                    hop(p, d, way).wait_send()
+
         return carry
 
     lax.fori_loop(0, pairs, finish, 0)
+    store.wait()
 
 
 def on_device(n_head, n_dp, queries, out_grad, latent, w_uk, w_uv, lengths, rewards, pairing):
@@ -227,6 +286,7 @@
     rows = D_C // n_dp
     vmem = pl.BlockSpec(memory_space=pltpu.VMEM)
     smem = pl.BlockSpec(memory_space=pltpu.SMEM)
+    hbm = pl.BlockSpec(memory_space=pl.ANY)
     q_grad, latent_grad, uk_grad, uv_grad = pl.pallas_call(
         functools.partial(kernel, n_head, n_dp, pairs),
         out_shape=(
@@ -235,23 +295,29 @@
             jax.ShapeDtypeStruct((rows, key_width), F32),
             jax.ShapeDtypeStruct((rows, key_width), F32),
         ),
-        in_specs=[smem] * 3 + [vmem] * 5,
-        out_specs=(vmem,) * 4,
+        in_specs=[smem] * 3 + [vmem] + [hbm] * 4,
+        out_specs=(hbm, vmem, vmem, vmem),
         scratch_shapes=[
+            pltpu.VMEM((length_all, q_width), BF16),
+            pltpu.VMEM((length_all, key_width), BF16),
+            pltpu.VMEM((D_C, key_width), BF16),
+            pltpu.VMEM((D_C, key_width), BF16),
+            pltpu.VMEM((length_all, q_width), BF16),
             pltpu.VMEM((length_all, D_C + D_R), BF16),
             pltpu.VMEM((D_C, length_all), BF16),
             pltpu.VMEM((pairs, n_dp, rows, 2 * DN + 2 * DV), BF16),
-            pltpu.VMEM((pairs, n_dp - 1, rows, 2 * DN + 2 * DV), BF16),
+            pltpu.VMEM((pairs, 2, n_dp, rows, 2 * DN + 2 * DV), BF16),
             pltpu.VMEM((pairs, length_all, 2 * DN + 2 * DV), BF16),
             pltpu.VMEM((length_all, 2 * DN), F32),
             pltpu.VMEM((n_head, tokens, D_C + D_R), F32),
             pltpu.VMEM((n_head - 1, tokens, D_C + D_R), F32),
             pltpu.SemaphoreType.DMA((n_head - 1,)),
             pltpu.SemaphoreType.DMA((n_head - 1,)),
-            pltpu.SemaphoreType.DMA((pairs, n_dp - 1)),
-            pltpu.SemaphoreType.DMA((pairs, n_dp - 1)),
+            pltpu.SemaphoreType.DMA((pairs, n_dp)),
+            pltpu.SemaphoreType.DMA((pairs, 2, n_dp)),
             pltpu.SemaphoreType.DMA((n_head - 1,)),
             pltpu.SemaphoreType.DMA((n_head - 1,)),
+            pltpu.SemaphoreType.DMA((4,)),
         ],
         compiler_params=pltpu.CompilerParams(
             collective_id=0, has_side_effects=True, vmem_limit_bytes=52 * 1024 * 1024

time: 122 us -> 106 us (0.87)
  the two profiles are of different devices: /device:TPU:9 before, /device:TPU:6 now
where the time goes in v2:
time: 106 us
  Pallas kernels  95.7 us (90%)
  local copies, waits for them, and re-layouts  8.95 us (8%)
  between operations  1.3 us (1%)
    pallas_call x1, Pallas kernels, on_device(): pl.pallas_call(functools.partial(kernel, n_head, n_dp, pairs), out_shape=...  95.7 us
    unnamed x11, local copies, waits for them, and re-layouts  8.95 us

profile of v2, /device:TPU:6, one launch (start us, length us, event | category | flops | bytes accessed | tf_op | source)
XLA Modules:
  0.0 106.0 jit_solution(8961524924630357068)
XLA Ops:
  1.3 1.1 %copy.12 = bf16[1,128,576]{2,1,0:T(8,128)(2,1)S(1)} copy(bf16[1,128,576]{1,2,0:T(8,128)(2,1)} %param.10) | data formatting | bytes 294912 | tf_op args[2]
  2.3 0.0 copy-start
  2.4 0.6 copy-done
  3.0 0.0 copy-start.1
  3.0 0.7 copy-done.1
  3.7 95.7 %shard_map.111 = (bf16[512,3072]{1,0:T(8,128)(2,1)}, bf16[128,576]{1,0:T(8,128)(2,1)S(1)}, f32[128,2048]{1,0:T(8,128)S(1)}, f32[128,2048]{1,0:T(8,128)}) custom-call(s32[1]{0:T(128)S(6)} %copy.17.lengths, f32[4]{0:T(128)S(1)} %copy-done, s32[4]{0:T(128)S(1)} %copy-done.1, bf16[128,576]{1,0:T(8,128)(2,1)S(1)} %bitcast.5, bf16[512,3072]{1,0:T(8,128)(2,1)} %bitcast.7, ...), custom_call_target="tpu_custom_call" | custom-call | tf_op jit(solution)/shard_map/pallas_call | solution.py:290
  99.4 0.8 copy.13
  100.2 0.0 copy-start.2
  100.2 3.8 %copy.18 = bf16[1,512,3072]{2,1,0:T(8,128)(2,1)} copy(bf16[1,512,3072]{2,1,0:T(8,128)(2,1)} %bitcast.8) | data formatting | bytes 6291456
  104.0 1.0 copy.19
  105.0 0.0 copy-done.2
  105.0 1.0 copy.20
Async XLA Ops:
  2.3 0.7 copy-start
  3.0 0.7 copy-start.1
  100.2 4.8 %copy-start.2 = (f32[128,2048]{1,0:T(8,128)S(1)}, f32[128,2048]{1,0:T(8,128)}, u32[]{:S(2)}) copy-start(f32[128,2048]{1,0:T(8,128)} %get-tuple-element.23) | copy-start | bytes 3145732

commit v3 on v2

--- a/solution.py
+++ b/solution.py
@@ -48,7 +48,7 @@
     n_head, n_dp, pairs,
     lengths, rewards, pairing, latent, q_in, og_in, wk_in, wv_in,
     qg_out, lg, uk, uv,
-    q, og, wk, wv, qg, full, cont_t, send, recv, dkv, rope_acc, lacc, lrecv,
+    q, og, wk, wv, qg, full, cont_t, send, recv, dkv, rope_acc, lacc, lsend, lrecv,
     g_send, g_recv, p_send, p_recv, l_send, l_recv, load_sem,
 ):
     factor = (DN + D_R) ** (-0.5)
@@ -115,12 +115,12 @@
                 hop(p, d, way).start()
 
     place = (me_d, n_dp - 1 - me_d)
-    lags = tuple(at + (at + n_dp - 1) // n_dp for at in place)
+    lags = tuple(at + 0 for at in place)
 
     def latent_part(o):
         peer = lax.rem(me_h + o, n_head)
         return pltpu.make_async_remote_copy(
-            src_ref=lacc.at[peer],
+            src_ref=lsend.at[peer],
             dst_ref=lrecv.at[o - 1],
             send_sem=l_send.at[o - 1],
             recv_sem=l_recv.at[o - 1],
@@ -237,6 +237,7 @@
         return carry
 
     lax.fori_loop(0, pairs, back, 0)
+    lsend[...] = lacc[...].astype(BF16)
     for o in range(1, n_head):
         latent_part(o).start()
     for p in range(pairs - last, pairs):
@@ -249,7 +250,7 @@
     total = lacc[me_h]
     for o in range(1, n_head):
         latent_part(o).wait()
-        total = total + lrecv[o - 1]
+        total = total + lrecv[o - 1].astype(F32)
     lg[...] = total.astype(BF16)
 
     def finish(p, carry):
@@ -310,7 +311,8 @@
             pltpu.VMEM((pairs, length_all, 2 * DN + 2 * DV), BF16),
             pltpu.VMEM((length_all, 2 * DN), F32),
             pltpu.VMEM((n_head, tokens, D_C + D_R), F32),
-            pltpu.VMEM((n_head - 1, tokens, D_C + D_R), F32),
+            pltpu.VMEM((n_head, tokens, D_C + D_R), BF16),
+            pltpu.VMEM((n_head - 1, tokens, D_C + D_R), BF16),
             pltpu.SemaphoreType.DMA((n_head - 1,)),
             pltpu.SemaphoreType.DMA((n_head - 1,)),
             pltpu.SemaphoreType.DMA((pairs, n_dp)),

time: 106 us -> 105 us (level)
  no operation moved by 1% of the time
where the time goes in v3:
time: 105 us
  Pallas kernels  94.9 us (90%)
  local copies, waits for them, and re-layouts  8.95 us (9%)
  between operations  1.3 us (1%)
    pallas_call x1, Pallas kernels, on_device(): pl.pallas_call(functools.partial(kernel, n_head, n_dp, pairs), out_shape=...  94.9 us
    unnamed x11, local copies, waits for them, and re-layouts  8.95 us

profile of v3, /device:TPU:6, one launch (start us, length us, event | category | flops | bytes accessed | tf_op | source)
XLA Modules:
  0.0 105.2 jit_solution(4954166679234980330)
XLA Ops:
  1.3 1.1 %copy.12 = bf16[1,128,576]{2,1,0:T(8,128)(2,1)S(1)} copy(bf16[1,128,576]{1,2,0:T(8,128)(2,1)} %param.10) | data formatting | bytes 294912 | tf_op args[2]
  2.3 0.0 copy-start
  2.4 0.6 copy-done
  3.0 0.0 copy-start.1
  3.0 0.7 copy-done.1
  3.7 94.9 %shard_map.111 = (bf16[512,3072]{1,0:T(8,128)(2,1)}, bf16[128,576]{1,0:T(8,128)(2,1)S(1)}, f32[128,2048]{1,0:T(8,128)S(1)}, f32[128,2048]{1,0:T(8,128)}) custom-call(s32[1]{0:T(128)S(6)} %copy.17.lengths, f32[4]{0:T(128)S(1)} %copy-done, s32[4]{0:T(128)S(1)} %copy-done.1, bf16[128,576]{1,0:T(8,128)(2,1)S(1)} %bitcast.5, bf16[512,3072]{1,0:T(8,128)(2,1)} %bitcast.7, ...), custom_call_target="tpu_custom_call" | custom-call | tf_op jit(solution)/shard_map/pallas_call | solution.py:291
  98.6 0.8 copy.13
  99.4 0.0 copy-start.2
  99.4 3.8 %copy.18 = bf16[1,512,3072]{2,1,0:T(8,128)(2,1)} copy(bf16[1,512,3072]{2,1,0:T(8,128)(2,1)} %bitcast.8) | data formatting | bytes 6291456
  103.2 1.0 copy.19
  104.2 0.0 copy-done.2
  104.2 1.0 copy.20
Async XLA Ops:
  2.3 0.7 copy-start
  3.0 0.7 copy-start.1
  99.4 4.8 %copy-start.2 = (f32[128,2048]{1,0:T(8,128)S(1)}, f32[128,2048]{1,0:T(8,128)}, u32[]{:S(2)}) copy-start(f32[128,2048]{1,0:T(8,128)} %get-tuple-element.23) | copy-start | bytes 3145732

commit v4 on v3

--- a/solution.py
+++ b/solution.py
@@ -240,19 +240,6 @@
     lsend[...] = lacc[...].astype(BF16)
     for o in range(1, n_head):
         latent_part(o).start()
-    for p in range(pairs - last, pairs):
-        for way in range(2):
-
-            @pl.when(p + lags[way] >= pairs)
-            def _():
-                forward(p, way)
-
-    total = lacc[me_h]
-    for o in range(1, n_head):
-        latent_part(o).wait()
-        total = total + lrecv[o - 1].astype(F32)
-    lg[...] = total.astype(BF16)
-
     def finish(p, carry):
         cols = pl.ds(pl.multiple_of(p * 2 * DN, 2 * DN), 2 * DN)
         total = send[p, me_d].astype(F32)
@@ -275,7 +262,22 @@
 
         return carry
 
-    lax.fori_loop(0, pairs, finish, 0)
+    for p in range(pairs - last, pairs):
+        if p == pairs - 1:
+            lax.fori_loop(0, pairs - last, finish, 0)
+        for way in range(2):
+
+            @pl.when(p + lags[way] >= pairs)
+            def _():
+                forward(p, way)
+
+    total = lacc[me_h]
+    for o in range(1, n_head):
+        latent_part(o).wait()
+        total = total + lrecv[o - 1].astype(F32)
+    lg[...] = total.astype(BF16)
+
+    lax.fori_loop(pairs - last, pairs, finish, 0)
     store.wait()
 
 

time: 105 us -> 105 us (level)
  no operation moved by 1% of the time
where the time goes in v4:
time: 105 us
  Pallas kernels  94.9 us (90%)
  local copies, waits for them, and re-layouts  8.95 us (9%)
  between operations  1.3 us (1%)
    pallas_call x1, Pallas kernels, on_device(): pl.pallas_call(functools.partial(kernel, n_head, n_dp, pairs), out_shape=...  94.9 us
    unnamed x11, local copies, waits for them, and re-layouts  8.95 us

profile of v4, /device:TPU:6, one launch (start us, length us, event | category | flops | bytes accessed | tf_op | source)
XLA Modules:
  0.0 105.2 jit_solution(101818075617570249)
XLA Ops:
  1.3 1.1 %copy.12 = bf16[1,128,576]{2,1,0:T(8,128)(2,1)S(1)} copy(bf16[1,128,576]{1,2,0:T(8,128)(2,1)} %param.10) | data formatting | bytes 294912 | tf_op args[2]
  2.3 0.0 copy-start
  2.4 0.6 copy-done
  3.0 0.0 copy-start.1
  3.0 0.7 copy-done.1
  3.7 94.9 %shard_map.111 = (bf16[512,3072]{1,0:T(8,128)(2,1)}, bf16[128,576]{1,0:T(8,128)(2,1)S(1)}, f32[128,2048]{1,0:T(8,128)S(1)}, f32[128,2048]{1,0:T(8,128)}) custom-call(s32[1]{0:T(128)S(6)} %copy.17.lengths, f32[4]{0:T(128)S(1)} %copy-done, s32[4]{0:T(128)S(1)} %copy-done.1, bf16[128,576]{1,0:T(8,128)(2,1)S(1)} %bitcast.5, bf16[512,3072]{1,0:T(8,128)(2,1)} %bitcast.7, ...), custom_call_target="tpu_custom_call" | custom-call | tf_op jit(solution)/shard_map/pallas_call | solution.py:293
  98.6 0.8 copy.13
  99.4 0.0 copy-start.2
  99.4 3.8 %copy.18 = bf16[1,512,3072]{2,1,0:T(8,128)(2,1)} copy(bf16[1,512,3072]{2,1,0:T(8,128)(2,1)} %bitcast.8) | data formatting | bytes 6291456
  103.2 1.0 copy.19
  104.2 0.0 copy-done.2
  104.2 1.0 copy.20
Async XLA Ops:
  2.3 0.7 copy-start
  3.0 0.7 copy-start.1
  99.4 4.8 %copy-start.2 = (f32[128,2048]{1,0:T(8,128)S(1)}, f32[128,2048]{1,0:T(8,128)}, u32[]{:S(2)}) copy-start(f32[128,2048]{1,0:T(8,128)} %get-tuple-element.23) | copy-start | bytes 3145732
